TPU v7x, 32 devices: a whole 2x2x4 slice. The times are simulated.
32 devices in a mesh: row: 4 (over z), col: 8 (over y, x, core).
Axes of the slice: x: 2, y: 2, z: 4, core: 2. Of those that a mesh axis runs over, the one named last changes fastest.
Arguments:
- vectors: bfloat16 [16384, 256], P(('row', 'col')), may hold values from -6 to 6
- blocks: bfloat16 [4, 8, 256, 128, 128], P('row', 'col'), may hold values from -0.046875 to 0.046875
- block_rows: int32 [4, 8, 256], P('row', 'col'), may hold values from 0 to 31
- block_cols: int32 [4, 8, 256], P('row', 'col'), may hold values from 0 to 15
- block_count: int32 [4, 8], P('row', 'col'), may hold values from 32 to 256, as said below
- lower_edge: float32 [1], replicated, may hold values from -0.6 to -0.3
- upper_edge: float32 [1], replicated, may hold values from 1 to 2
Outputs:
- filtered: float32 [16384, 256], P(('row', 'col'))
Inputs may be any that keep to these rules, and one draw needn't show every extreme that they name: `block_count`: some device has all 256 slots live.
All inputs are finite; a program needn't handle non-finite values.
Results may differ from a plain program's by a relative error of at most 0.008.
Values may be sent and summed in bfloat16 or wider, within the bound.
A program may use at most 192 MiB of HBM per device.

v0:
```python
import jax
import jax.numpy as jnp
from jax import lax
from jax.sharding import PartitionSpec as P

DEGREE = 2


def pick_table(indices, count):
    return (indices[:, None] == jnp.arange(count, dtype=jnp.int32)[None, :]).astype(jnp.bfloat16)


def place_sum(table, values):
    upper = values.astype(jnp.bfloat16)
    lower = (values - upper.astype(jnp.float32)).astype(jnp.bfloat16)
    first = jnp.einsum("gt,giv->tiv", table, upper, preferred_element_type=jnp.float32)
    second = jnp.einsum("gt,giv->tiv", table, lower, preferred_element_type=jnp.float32)
    return first + second


def slot_products(
    local_blocks, local_rows, local_cols, slot_count, rows_side, cols_side, group_size, group_limit
):
    block_size = local_blocks.shape[1]
    vec_width = rows_side.shape[1]
    row_tiles = rows_side.reshape(-1, block_size, vec_width)
    col_tiles = cols_side.reshape(-1, block_size, vec_width)
    row_count = row_tiles.shape[0]
    col_count = col_tiles.shape[0]

    def group_step(position, totals):
        row_totals, col_totals = totals
        first_slot = position * group_size
        block_tile = lax.dynamic_slice_in_dim(local_blocks, first_slot, group_size, 0)
        rows_here = lax.dynamic_slice_in_dim(local_rows, first_slot, group_size, 0)
        cols_here = lax.dynamic_slice_in_dim(local_cols, first_slot, group_size, 0)
        live_mask = (first_slot + jnp.arange(group_size) < slot_count).astype(jnp.float32)[
            :, None, None
        ]
        row_table = pick_table(rows_here, row_count)
        col_table = pick_table(cols_here, col_count)
        col_picked = jnp.einsum(
            "gt,tjv->gjv", col_table, col_tiles, preferred_element_type=jnp.float32
        ).astype(jnp.bfloat16)
        row_picked = jnp.einsum(
            "gt,tjv->gjv", row_table, row_tiles, preferred_element_type=jnp.float32
        ).astype(jnp.bfloat16)
        forward = (
            jnp.einsum("gij,gjv->giv", block_tile, col_picked, preferred_element_type=jnp.float32)
            * live_mask
        )
        mirror = (
            jnp.einsum("gji,gjv->giv", block_tile, row_picked, preferred_element_type=jnp.float32)
            * live_mask
        )
        return (
            row_totals + place_sum(row_table, forward),
            col_totals + place_sum(col_table, mirror),
        )

    start_totals = (
        jnp.zeros(row_tiles.shape, jnp.float32),
        jnp.zeros(col_tiles.shape, jnp.float32),
    )
    row_totals, col_totals = lax.fori_loop(0, group_limit, group_step, start_totals)
    return (row_totals.reshape(-1, vec_width), col_totals.reshape(-1, vec_width))


def per_device(vectors, blocks, block_rows, block_cols, block_count, lower_edge, upper_edge):
    center = (upper_edge[0] + lower_edge[0]) * 0.5
    half_width = (upper_edge[0] - lower_edge[0]) * 0.5
    local_blocks = blocks[0, 0]
    local_rows = block_rows[0, 0]
    local_cols = block_cols[0, 0]
    slot_count = block_count[0, 0]
    group_size = min(64, local_blocks.shape[0])
    group_limit = local_blocks.shape[0] // group_size
    current = vectors.astype(jnp.float32)
    previous = jnp.zeros_like(current)
    for degree in range(DEGREE):
        operand = current.astype(jnp.bfloat16)
        cols_side = lax.all_gather(operand, "row", axis=0, tiled=True)
        rows_side = lax.all_gather(operand, "col", axis=0, tiled=True)
        row_part, col_part = slot_products(
            local_blocks,
            local_rows,
            local_cols,
            slot_count,
            rows_side,
            cols_side,
            group_size,
            group_limit,
        )
        forward = lax.psum_scatter(row_part, "col", scatter_dimension=0, tiled=True)
        applied = forward + lax.psum_scatter(col_part, "row", scatter_dimension=0, tiled=True)
        shifted = applied - center * current
        if degree == 0:
            following = shifted / half_width
        else:
            following = 2.0 * shifted / half_width - previous
        previous, current = (current, following)
    return current


def solution(mesh):
    return jax.shard_map(
        per_device,
        mesh=mesh,
        in_specs=(
            P(("row", "col"), None),
            P("row", "col", None, None, None),
            P("row", "col", None),
            P("row", "col", None),
            P("row", "col"),
            P(),
            P(),
        ),
        out_specs=P(("row", "col"), None),
        check_vma=False,
    )
```

profile of v0, /device:TPU:0, one launch (start us, length us, event | category | flops | bytes accessed | tf_op | source)
XLA Modules:
  0.0 725.1 jit_solution(12272732270687093132)
XLA Ops:
  8.1 31.5 %all-gather.5.cloned.1.call-done = bf16[2048,256]{1,0:T(8,128)(2,1)} async-done(((bf16[512,256]{1,0:T(8,128)(2,1)}), bf16[2048,256]{1,0:T(8,128)(2,1)}) %all-gather.5.cloned.1.call-update) | async-done | bytes 1048592 | tf_op jit(solution)/shard_map/all_gather | solution.py:82
  39.6 29.3 %all-gather.7.cloned.1.call-done = bf16[4096,256]{1,0:T(8,128)(2,1)} async-done(((bf16[512,256]{1,0:T(8,128)(2,1)}), bf16[4096,256]{1,0:T(8,128)(2,1)}) %all-gather.7.cloned.1.call-update) | async-done | bytes 2097168 | tf_op jit(solution)/shard_map/all_gather | solution.py:83
  68.9 192.4 %while.32 = (s32[]{:T(128)}, f32[32,128,256]{2,0,1:T(8,128)}, f32[16,128,256]{2,0,1:T(8,128)}, s32[256]{0:T(256)}, bf16[256,128,128]{2,1,0:T(8,128)(2,1)}, /*ind...) while((s32[]{:T(128)}, f32[32,128,256]{2,0,1:T(8,128)}, ...), condition=%wide.region_1.0_spmd.clone, body=%wide.region_0.0_spmd.clone.sunk | while | flops 1703421184 | bytes 141565264 | solution.py:65
  72.2 8.0 %fusion.125 = f32[64,128,256]{2,1,0:T(8,128)} fusion(bf16[64,128,256]{2,0,1:T(8,128)(2,1)S(1)} %fusion.124, bf16[256,128,128]{2,1,0:T(8,128)(2,1)} %get-tuple-element.583, s32[]{:T(128)S(6)} %select_n.22), kind=kOutput, calls=%fused_computation.6.clone.1 | convolution fusion | flops 536870912 | bytes 14680068 | tf_op jit(solution)/shard_map/while/body/eval_jaxpr/gij,gjv->giv/dot_general | solution.py:49
  82.5 13.0 %multiply_convert_fusion.6 = (bf16[64,128,256]{2,1,0:T(8,128)(2,1)}, bf16[64,128,256]{2,1,0:T(8,128)(2,1)}, bf16[64,128,256]{2,1,0:T(8,128)(2,1)}, bf16[64,128,256]{2,1,0:T(8,128)(2,1)}) fusion(f32[64]{0:T(128)S(1)} %compare_convert_fusion.4, f32[64,128,256]{2,1,0:T(8,128)} %fusion.125, bf16[64,128,256]{2,0,1:T(8,128)(2,1)S(1)} %fusion.126, ...), kind=kOutput, calls=%fused_computation.4.clone.2 | convolution fusion | flops 557842432 | bytes 31457540 | tf_op jit(solution)/shard_map/while/body/eval_jaxpr/gji,gjv->giv/dot_general | solution.py:53
  118.1 8.0 %fusion.125 = f32[64,128,256]{2,1,0:T(8,128)} fusion(bf16[64,128,256]{2,0,1:T(8,128)(2,1)S(1)} %fusion.124, bf16[256,128,128]{2,1,0:T(8,128)(2,1)} %get-tuple-element.583, s32[]{:T(128)S(6)} %select_n.22), kind=kOutput, calls=%fused_computation.6.clone.1 | convolution fusion | flops 536870912 | bytes 14680068 | tf_op jit(solution)/shard_map/while/body/eval_jaxpr/gij,gjv->giv/dot_general | solution.py:49
  128.3 13.0 %multiply_convert_fusion.6 = (bf16[64,128,256]{2,1,0:T(8,128)(2,1)}, bf16[64,128,256]{2,1,0:T(8,128)(2,1)}, bf16[64,128,256]{2,1,0:T(8,128)(2,1)}, bf16[64,128,256]{2,1,0:T(8,128)(2,1)}) fusion(f32[64]{0:T(128)S(1)} %compare_convert_fusion.4, f32[64,128,256]{2,1,0:T(8,128)} %fusion.125, bf16[64,128,256]{2,0,1:T(8,128)(2,1)S(1)} %fusion.126, ...), kind=kOutput, calls=%fused_computation.4.clone.2 | convolution fusion | flops 557842432 | bytes 31457540 | tf_op jit(solution)/shard_map/while/body/eval_jaxpr/gji,gjv->giv/dot_general | solution.py:53
  166.8 8.0 %fusion.125 = f32[64,128,256]{2,1,0:T(8,128)} fusion(bf16[64,128,256]{2,0,1:T(8,128)(2,1)S(1)} %fusion.124, bf16[256,128,128]{2,1,0:T(8,128)(2,1)} %get-tuple-element.583, s32[]{:T(128)S(6)} %select_n.22), kind=kOutput, calls=%fused_computation.6.clone.1 | convolution fusion | flops 536870912 | bytes 14680068 | tf_op jit(solution)/shard_map/while/body/eval_jaxpr/gij,gjv->giv/dot_general | solution.py:49
  177.1 13.0 %multiply_convert_fusion.6 = (bf16[64,128,256]{2,1,0:T(8,128)(2,1)}, bf16[64,128,256]{2,1,0:T(8,128)(2,1)}, bf16[64,128,256]{2,1,0:T(8,128)(2,1)}, bf16[64,128,256]{2,1,0:T(8,128)(2,1)}) fusion(f32[64]{0:T(128)S(1)} %compare_convert_fusion.4, f32[64,128,256]{2,1,0:T(8,128)} %fusion.125, bf16[64,128,256]{2,0,1:T(8,128)(2,1)S(1)} %fusion.126, ...), kind=kOutput, calls=%fused_computation.4.clone.2 | convolution fusion | flops 557842432 | bytes 31457540 | tf_op jit(solution)/shard_map/while/body/eval_jaxpr/gji,gjv->giv/dot_general | solution.py:53
  215.5 8.0 %fusion.125 = f32[64,128,256]{2,1,0:T(8,128)} fusion(bf16[64,128,256]{2,0,1:T(8,128)(2,1)S(1)} %fusion.124, bf16[256,128,128]{2,1,0:T(8,128)(2,1)} %get-tuple-element.583, s32[]{:T(128)S(6)} %select_n.22), kind=kOutput, calls=%fused_computation.6.clone.1 | convolution fusion | flops 536870912 | bytes 14680068 | tf_op jit(solution)/shard_map/while/body/eval_jaxpr/gij,gjv->giv/dot_general | solution.py:49
  225.8 13.0 %multiply_convert_fusion.6 = (bf16[64,128,256]{2,1,0:T(8,128)(2,1)}, bf16[64,128,256]{2,1,0:T(8,128)(2,1)}, bf16[64,128,256]{2,1,0:T(8,128)(2,1)}, bf16[64,128,256]{2,1,0:T(8,128)(2,1)}) fusion(f32[64]{0:T(128)S(1)} %compare_convert_fusion.4, f32[64,128,256]{2,1,0:T(8,128)} %fusion.125, bf16[64,128,256]{2,0,1:T(8,128)(2,1)S(1)} %fusion.126, ...), kind=kOutput, calls=%fused_computation.4.clone.2 | convolution fusion | flops 557842432 | bytes 31457540 | tf_op jit(solution)/shard_map/while/body/eval_jaxpr/gji,gjv->giv/dot_general | solution.py:53
  273.5 36.0 %reduce-scatter.7.cloned.1.call-done = f32[512,256]{1,0:T(8,128)} async-done(((f32[2048,256]{1,0:T(8,128)}), f32[512,256]{1,0:T(8,128)}) %reduce-scatter.7.cloned.1.call-update) | async-done | bytes 524304 | tf_op jit(solution)/shard_map/reduce_scatter | solution.py:95
  309.5 54.2 %reduce-scatter.5.cloned.1.call-done = f32[512,256]{1,0:T(8,128)} async-done(((f32[4096,256]{1,0:T(8,128)}), f32[512,256]{1,0:T(8,128)}) %reduce-scatter.5.cloned.1.call-update) | async-done | bytes 524304 | tf_op jit(solution)/shard_map/reduce_scatter | solution.py:94
  366.4 27.4 %all-gather.9.cloned.1.call-done = bf16[2048,256]{1,0:T(8,128)(2,1)} async-done(((bf16[512,256]{1,0:T(8,128)(2,1)}), bf16[2048,256]{1,0:T(8,128)(2,1)}) %all-gather.9.cloned.1.call-update) | async-done | bytes 1048592 | tf_op jit(solution)/shard_map/all_gather | solution.py:82
  393.8 29.2 %all-gather.11.cloned.1.call-done = bf16[4096,256]{1,0:T(8,128)(2,1)} async-done(((bf16[512,256]{1,0:T(8,128)(2,1)}), bf16[4096,256]{1,0:T(8,128)(2,1)}) %all-gather.11.cloned.1.call-update) | async-done | bytes 2097168 | tf_op jit(solution)/shard_map/all_gather | solution.py:83
  423.0 190.0 %while.33 = (s32[]{:T(128)}, f32[32,128,256]{2,0,1:T(8,128)}, f32[16,128,256]{2,0,1:T(8,128)}, s32[256]{0:T(256)S(1)}, bf16[256,128,128]{2,1,0:T(8,128)(2,1)}, /...) while((s32[]{:T(128)}, f32[32,128,256]{2,0,1:T(8,128)}, ...), condition=%wide.region_5.0_spmd.clone, body=%wide.region_4.0_spmd.clone.sunk | while | flops 1703421184 | bytes 141561136 | solution.py:65
  425.8 8.0 %fusion.143 = f32[64,128,256]{2,1,0:T(8,128)} fusion(bf16[64,128,256]{2,0,1:T(8,128)(2,1)S(1)} %fusion.142, bf16[256,128,128]{2,1,0:T(8,128)(2,1)} %get-tuple-element.622, s32[]{:T(128)S(6)} %select_n.23), kind=kOutput, calls=%fused_computation.43.clone.1 | convolution fusion | flops 536870912 | bytes 14680068 | tf_op jit(solution)/shard_map/while/body/eval_jaxpr/gij,gjv->giv/dot_general | solution.py:49
  436.0 13.1 %multiply_convert_fusion.7 = (bf16[64,128,256]{2,1,0:T(8,128)(2,1)}, bf16[64,128,256]{2,1,0:T(8,128)(2,1)}, bf16[64,128,256]{2,1,0:T(8,128)(2,1)}, bf16[64,128,256]{2,1,0:T(8,128)(2,1)}) fusion(f32[64]{0:T(128)S(1)} %compare_convert_fusion.5, f32[64,128,256]{2,1,0:T(8,128)} %fusion.143, bf16[64,128,256]{2,0,1:T(8,128)(2,1)S(1)} %fusion.144, ...), kind=kOutput, calls=%fused_computation.41.clone.2 | convolution fusion | flops 557842432 | bytes 31457540 | tf_op jit(solution)/shard_map/while/body/eval_jaxpr/gji,gjv->giv/dot_general | solution.py:53
  471.0 8.0 %fusion.143 = f32[64,128,256]{2,1,0:T(8,128)} fusion(bf16[64,128,256]{2,0,1:T(8,128)(2,1)S(1)} %fusion.142, bf16[256,128,128]{2,1,0:T(8,128)(2,1)} %get-tuple-element.622, s32[]{:T(128)S(6)} %select_n.23), kind=kOutput, calls=%fused_computation.43.clone.1 | convolution fusion | flops 536870912 | bytes 14680068 | tf_op jit(solution)/shard_map/while/body/eval_jaxpr/gij,gjv->giv/dot_general | solution.py:49
  481.3 13.1 %multiply_convert_fusion.7 = (bf16[64,128,256]{2,1,0:T(8,128)(2,1)}, bf16[64,128,256]{2,1,0:T(8,128)(2,1)}, bf16[64,128,256]{2,1,0:T(8,128)(2,1)}, bf16[64,128,256]{2,1,0:T(8,128)(2,1)}) fusion(f32[64]{0:T(128)S(1)} %compare_convert_fusion.5, f32[64,128,256]{2,1,0:T(8,128)} %fusion.143, bf16[64,128,256]{2,0,1:T(8,128)(2,1)S(1)} %fusion.144, ...), kind=kOutput, calls=%fused_computation.41.clone.2 | convolution fusion | flops 557842432 | bytes 31457540 | tf_op jit(solution)/shard_map/while/body/eval_jaxpr/gji,gjv->giv/dot_general | solution.py:53
  529.4 13.1 %multiply_convert_fusion.7 = (bf16[64,128,256]{2,1,0:T(8,128)(2,1)}, bf16[64,128,256]{2,1,0:T(8,128)(2,1)}, bf16[64,128,256]{2,1,0:T(8,128)(2,1)}, bf16[64,128,256]{2,1,0:T(8,128)(2,1)}) fusion(f32[64]{0:T(128)S(1)} %compare_convert_fusion.5, f32[64,128,256]{2,1,0:T(8,128)} %fusion.143, bf16[64,128,256]{2,0,1:T(8,128)(2,1)S(1)} %fusion.144, ...), kind=kOutput, calls=%fused_computation.41.clone.2 | convolution fusion | flops 557842432 | bytes 31457540 | tf_op jit(solution)/shard_map/while/body/eval_jaxpr/gji,gjv->giv/dot_general | solution.py:53
  577.5 13.1 %multiply_convert_fusion.7 = (bf16[64,128,256]{2,1,0:T(8,128)(2,1)}, bf16[64,128,256]{2,1,0:T(8,128)(2,1)}, bf16[64,128,256]{2,1,0:T(8,128)(2,1)}, bf16[64,128,256]{2,1,0:T(8,128)(2,1)}) fusion(f32[64]{0:T(128)S(1)} %compare_convert_fusion.5, f32[64,128,256]{2,1,0:T(8,128)} %fusion.143, bf16[64,128,256]{2,0,1:T(8,128)(2,1)S(1)} %fusion.144, ...), kind=kOutput, calls=%fused_computation.41.clone.2 | convolution fusion | flops 557842432 | bytes 31457540 | tf_op jit(solution)/shard_map/while/body/eval_jaxpr/gji,gjv->giv/dot_general | solution.py:53
  623.9 37.4 %reduce-scatter.11.cloned.1.call-done = f32[512,256]{1,0:T(8,128)} async-done(((f32[2048,256]{1,0:T(8,128)}), f32[512,256]{1,0:T(8,128)}) %reduce-scatter.11.cloned.1.call-update) | async-done | bytes 524304 | tf_op jit(solution)/shard_map/reduce_scatter | solution.py:95
  661.3 54.4 %reduce-scatter.9.cloned.1.call-done = f32[512,256]{1,0:T(8,128)} async-done(((f32[4096,256]{1,0:T(8,128)}), f32[512,256]{1,0:T(8,128)}) %reduce-scatter.9.cloned.1.call-update) | async-done | bytes 524304 | tf_op jit(solution)/shard_map/reduce_scatter | solution.py:94
  (166 shorter events, 257.0 us)
Async XLA Ops:
  6.5 33.1 %all-gather.5.cloned.1.call-start = ((), (), s32[]{:S(2)}) async-start(), calls=%async_computation.4 | async-start | bytes 1310720 | tf_op jit(solution)/shard_map/all_gather | solution.py:82
  7.3 61.6 %all-gather.7.cloned.1.call-start = ((), (), s32[]{:S(2)}) async-start(), calls=%async_computation.5 | async-start | bytes 2359296 | tf_op jit(solution)/shard_map/all_gather | solution.py:83
  8.0 301.5 %reduce-scatter.7.cloned.1.call-start = ((), (), s32[]{:S(2)}) async-start(), calls=%async_computation.7 | async-start | bytes 2621440 | tf_op jit(solution)/shard_map/reduce_scatter | solution.py:95
  72.2 8.0 %copy-start.9 = (s32[256]{0:T(256)S(1)}, s32[256]{0:T(256)}, u32[]{:S(2)}) copy-start(s32[256]{0:T(256)} %get-tuple-element.582) | copy-start | bytes 3076 | tf_op jit(solution)/shard_map/while
  72.2 8.1 %copy-start.5 = (bf16[32,128,256]{2,1,0:T(8,128)(2,1)S(1)}, bf16[32,128,256]{2,1,0:T(8,128)(2,1)}, u32[]{:S(2)}) copy-start(bf16[32,128,256]{2,1,0:T(8,128)(2,1)} %get-tuple-element.587) | copy-start | bytes 6291460 | tf_op jit(solution)/shard_map/while
  118.1 8.0 %copy-start.9 = (s32[256]{0:T(256)S(1)}, s32[256]{0:T(256)}, u32[]{:S(2)}) copy-start(s32[256]{0:T(256)} %get-tuple-element.582) | copy-start | bytes 3076 | tf_op jit(solution)/shard_map/while
  118.1 8.1 %copy-start.5 = (bf16[32,128,256]{2,1,0:T(8,128)(2,1)S(1)}, bf16[32,128,256]{2,1,0:T(8,128)(2,1)}, u32[]{:S(2)}) copy-start(bf16[32,128,256]{2,1,0:T(8,128)(2,1)} %get-tuple-element.587) | copy-start | bytes 6291460 | tf_op jit(solution)/shard_map/while
  166.8 8.1 %copy-start.5 = (bf16[32,128,256]{2,1,0:T(8,128)(2,1)S(1)}, bf16[32,128,256]{2,1,0:T(8,128)(2,1)}, u32[]{:S(2)}) copy-start(bf16[32,128,256]{2,1,0:T(8,128)(2,1)} %get-tuple-element.587) | copy-start | bytes 6291460 | tf_op jit(solution)/shard_map/while
  215.5 8.0 %copy-start.9 = (s32[256]{0:T(256)S(1)}, s32[256]{0:T(256)}, u32[]{:S(2)}) copy-start(s32[256]{0:T(256)} %get-tuple-element.582) | copy-start | bytes 3076 | tf_op jit(solution)/shard_map/while
  215.5 8.1 %copy-start.5 = (bf16[32,128,256]{2,1,0:T(8,128)(2,1)S(1)}, bf16[32,128,256]{2,1,0:T(8,128)(2,1)}, u32[]{:S(2)}) copy-start(bf16[32,128,256]{2,1,0:T(8,128)(2,1)} %get-tuple-element.587) | copy-start | bytes 6291460 | tf_op jit(solution)/shard_map/while
  265.5 98.3 %reduce-scatter.5.cloned.1.call-start = ((), (), s32[]{:S(2)}) async-start(), calls=%async_computation.6 | async-start | bytes 4718592 | tf_op jit(solution)/shard_map/reduce_scatter | solution.py:94
  272.1 91.6 %copy-start.6 = (bf16[512,256]{1,0:T(8,128)(2,1)S(1)}, bf16[512,256]{1,0:T(8,128)(2,1)}, u32[]{:S(2)}) copy-start(bf16[512,256]{1,0:T(8,128)(2,1)} %param.11) | copy-start | bytes 786436
  272.1 150.9 %copy-start.10 = (s32[256]{0:T(256)S(1)}, s32[256]{0:T(256)}, u32[]{:S(2)}) copy-start(s32[256]{0:T(256)} %get-tuple-element.664) | copy-start | bytes 3076
  272.1 150.9 %copy-start.11 = (s32[256]{0:T(256)S(1)}, s32[256]{0:T(256)}, u32[]{:S(2)}) copy-start(s32[256]{0:T(256)} %get-tuple-element.665) | copy-start | bytes 3076
  272.1 121.7 %all-gather.9.cloned.1.call-start = ((), (), s32[]{:S(2)}) async-start(), calls=%async_computation.8 | async-start | bytes 1310720 | tf_op jit(solution)/shard_map/all_gather | solution.py:82
  365.8 57.2 %all-gather.11.cloned.1.call-start = ((), (), s32[]{:S(2)}) async-start(), calls=%async_computation.9 | async-start | bytes 2359296 | tf_op jit(solution)/shard_map/all_gather | solution.py:83
  366.3 294.9 %reduce-scatter.11.cloned.1.call-start = ((), (), s32[]{:S(2)}) async-start(), calls=%async_computation.11 | async-start | bytes 2621440 | tf_op jit(solution)/shard_map/reduce_scatter | solution.py:95
  425.8 8.1 %copy-start.4 = (bf16[32,128,256]{2,1,0:T(8,128)(2,1)S(1)}, bf16[32,128,256]{2,1,0:T(8,128)(2,1)}, u32[]{:S(2)}) copy-start(bf16[32,128,256]{2,1,0:T(8,128)(2,1)} %get-tuple-element.626) | copy-start | bytes 6291460 | tf_op jit(solution)/shard_map/while
  471.0 8.1 %copy-start.4 = (bf16[32,128,256]{2,1,0:T(8,128)(2,1)S(1)}, bf16[32,128,256]{2,1,0:T(8,128)(2,1)}, u32[]{:S(2)}) copy-start(bf16[32,128,256]{2,1,0:T(8,128)(2,1)} %get-tuple-element.626) | copy-start | bytes 6291460 | tf_op jit(solution)/shard_map/while
  519.2 8.1 %copy-start.4 = (bf16[32,128,256]{2,1,0:T(8,128)(2,1)S(1)}, bf16[32,128,256]{2,1,0:T(8,128)(2,1)}, u32[]{:S(2)}) copy-start(bf16[32,128,256]{2,1,0:T(8,128)(2,1)} %get-tuple-element.626) | copy-start | bytes 6291460 | tf_op jit(solution)/shard_map/while
  567.3 8.1 %copy-start.4 = (bf16[32,128,256]{2,1,0:T(8,128)(2,1)S(1)}, bf16[32,128,256]{2,1,0:T(8,128)(2,1)}, u32[]{:S(2)}) copy-start(bf16[32,128,256]{2,1,0:T(8,128)(2,1)} %get-tuple-element.626) | copy-start | bytes 6291460 | tf_op jit(solution)/shard_map/while
  617.2 98.5 %reduce-scatter.9.cloned.1.call-start = ((), (), s32[]{:S(2)}) async-start(), calls=%async_computation.10 | async-start | bytes 4718592 | tf_op jit(solution)/shard_map/reduce_scatter | solution.py:94
  623.8 91.8 %copy-start.7 = (f32[512,256]{1,0:T(8,128)S(1)}, f32[512,256]{1,0:T(8,128)}, u32[]{:S(2)}) copy-start(f32[512,256]{1,0:T(8,128)} %reduce-scatter.7.cloned.1.call-done) | copy-start | bytes 1572868
  623.8 91.8 %copy-start.8 = (f32[512,256]{1,0:T(8,128)S(1)}, f32[512,256]{1,0:T(8,128)}, u32[]{:S(2)}) copy-start(f32[512,256]{1,0:T(8,128)} %reduce-scatter.5.cloned.1.call-done) | copy-start | bytes 1572868
  (17 other events, 86.0 us)
Sparse Core Ops, SparseCore 0:
  8.9 30.6 all-gather.4
  41.5 27.3 all-gather.6
  265.6 43.8 reduce-scatter.6
  313.1 50.6 reduce-scatter.4
  365.9 27.8 all-gather.8
  395.6 27.3 all-gather.10
  617.3 43.8 reduce-scatter.10
  665.0 50.6 reduce-scatter.8
where the time goes:
time: 740 us; the launch traced here: 725 us
  matrix products  372 us (50%)
  waiting for transfers between devices  301 us (41%)
  local copies, waits for them, and re-layouts  25.5 us (3%)
  between operations  15.3 us (2%)
  other arithmetic  9.4 us (1%)
    dot_general x16, matrix products, place_sum(): jnp.einsum('gt,giv->tiv', table, upper, preferred_element_type=jnp.float32)  111 us
    reduce_scatter x2, waiting for transfers between devices, per_device(): forward = lax.psum_scatter(row_part, 'col', scatter_dimension=0, tiled=True)  109 us
    dot_general x8, matrix products, group_step(): jnp.einsum('gji,gjv->giv', block_tile, row_picked, preferred_element_type...  104 us
    reduce_scatter x2, waiting for transfers between devices, per_device(): lax.psum_scatter(col_part, 'row', scatter_dimension=0, tiled=True)  73.4 us
    dot_general x8, matrix products, group_step(): jnp.einsum('gij,gjv->giv', block_tile, col_picked, preferred_element_type...  64.1 us
    dot_general x16, matrix products, place_sum(): jnp.einsum('gt,giv->tiv', table, lower, preferred_element_type=jnp.float32)  60.6 us
    all_gather x2, waiting for transfers between devices, per_device(): cols_side = lax.all_gather(operand, 'row', axis=0, tiled=True)  58.9 us
    all_gather x2, waiting for transfers between devices, per_device(): rows_side = lax.all_gather(operand, 'col', axis=0, tiled=True)  58.5 us
  transfers between devices with their start and end apart: 8, of which 8 were waited for; matrix products, arithmetic and copies ran while one was open for 2% of the time, Pallas kernels for 0%

commit v1 on v0

--- a/solution.py
+++ b/solution.py
@@ -1,7 +1,13 @@
+import functools
+
 import jax
 import jax.numpy as jnp
 from jax import lax
+from jax.experimental import pallas as pl
+from jax.experimental.pallas import tpu as pltpu
 from jax.sharding import PartitionSpec as P
+
+MESH = pl.DeviceIdType.MESH
 
 DEGREE = 2
 
@@ -102,9 +108,442 @@
     return current
 
 
+def densify_kernel(rows_ref, cols_ref, count_ref, blocks_ref, dense_ref, head, follow):
+    col_segs, row_segs, seg, _ = dense_ref.shape
+    block = blocks_ref.shape[1]
+    per_seg = seg // block
+    col_blocks = row_segs * per_seg
+    count = count_ref[0, 0]
+
+    def clear_head(i, carry):
+        head[i] = -1
+        return carry
+
+    lax.fori_loop(0, head.shape[0], clear_head, 0, unroll=8)
+
+    def link(i, carry):
+        slot = count - 1 - i
+        place = rows_ref[slot] * col_blocks + cols_ref[slot]
+        follow[slot] = head[place]
+        head[place] = slot
+        return carry
+
+    lax.fori_loop(0, count, link, 0)
+
+    def clear(i, carry):
+        dense_ref[i // row_segs, i % row_segs] = jnp.zeros((seg, seg), dense_ref.dtype)
+        return carry
+
+    lax.fori_loop(0, col_segs * row_segs, clear, 0)
+
+    def place_slot(slot, carry):
+        row, col = rows_ref[slot], cols_ref[slot]
+        after = follow[slot]
+        is_first = head[row * col_blocks + col] == slot
+        target = dense_ref.at[
+            row // per_seg,
+            col // per_seg,
+            pl.ds(pl.multiple_of((row % per_seg) * block, block), block),
+            pl.ds(pl.multiple_of((col % per_seg) * block, block), block),
+        ]
+
+        @pl.when(is_first & (after < 0))
+        def _():
+            target[...] = blocks_ref[slot]
+
+        @pl.when(is_first & (after >= 0))
+        def _():
+            def more(state):
+                return state[0] >= 0
+
+            def add(state):
+                at, total = state
+                return follow[at], total + blocks_ref[at].astype(jnp.float32)
+
+            _, total = lax.while_loop(more, add, (after, blocks_ref[slot].astype(jnp.float32)))
+            target[...] = total.astype(dense_ref.dtype)
+
+        return carry
+
+    lax.fori_loop(0, count, place_slot, 0)
+
+
+def densify(blocks, block_rows, block_cols, block_count, row_segs, col_segs, seg):
+    slots, block, _ = blocks.shape
+    places = col_segs * row_segs * (seg // block) ** 2
+    return pl.pallas_call(
+        densify_kernel,
+        out_shape=jax.ShapeDtypeStruct((col_segs, row_segs, seg, seg), jnp.bfloat16),
+        in_specs=[pl.BlockSpec(memory_space=pltpu.SMEM)] * 3 + [pl.BlockSpec(memory_space=pltpu.VMEM)],
+        out_specs=pl.BlockSpec(memory_space=pltpu.VMEM),
+        scratch_shapes=[pltpu.SMEM((places,), jnp.int32), pltpu.SMEM((slots,), jnp.int32)],
+        compiler_params=pltpu.CompilerParams(vmem_limit_bytes=48 * 2**20),
+        name="densify",
+    )(block_rows, block_cols, block_count, blocks)
+
+
+GATHER = (
+    (0, None, 1), (0, None, 2), (0, None, 4),
+    (2, 0, 4), (4, 1, 2),
+    (2, None, 1), (4, None, 1),
+    (6, 0, 1), (6, 1, 1),
+)
+
+
+def filter_kernel(
+    n_row, n_col, x_ref, lower_ref, upper_ref, dense_hbm, out_ref,
+    dense, rows, cols, mirror_t, forward, current, previous,
+    core_out, core_in, diag_out, diag_in, quad_out, quad_in,
+    up_out, up_in, down_out, down_in,
+    dense_sem, gather_send, gather_recv, chain_up_send, chain_down_send, chain_recv,
+    core_send, core_recv, diag_send, diag_recv, quad_send, quad_recv,
+    up_send, up_recv, down_send, down_recv,
+):
+    seg = x_ref.shape[0]
+    half = seg // 2
+    halves = (pl.ds(0, half), pl.ds(half, half))
+    f32, bf16 = jnp.float32, jnp.bfloat16
+    r = lax.axis_index("row")
+    c = lax.axis_index("col")
+    core, along_x, along_y = c % 2, (c // 2) % 2, c // 4
+    has_up, has_down = r < n_row - 1, r > 0
+
+    def peer(j):
+        y = 1 - along_y if j & 4 else along_y
+        x = 1 - along_x if j & 2 else along_x
+        k = 1 - core if j & 1 else core
+        return y * 4 + x * 2 + k
+
+    def send(src, dst, send_sem, recv_sem, device):
+        return pltpu.make_async_remote_copy(
+            src_ref=src, dst_ref=dst, send_sem=send_sem, recv_sem=recv_sem,
+            device_id=device, device_id_type=MESH,
+        )
+
+    def dense_copy(j):
+        return pltpu.make_async_copy(dense_hbm.at[peer(j)], dense.at[peer(j)], dense_sem.at[j])
+
+    for j in range(n_col):
+        dense_copy(j).start()
+
+    barrier = pltpu.get_barrier_semaphore()
+    for j in (1, 2, 4):
+        pl.semaphore_signal(barrier, inc=1, device_id=(r, peer(j)), device_id_type=MESH)
+
+    @pl.when(has_up)
+    def _():
+        pl.semaphore_signal(barrier, inc=1, device_id=(r + 1, c), device_id_type=MESH)
+
+    @pl.when(has_down)
+    def _():
+        pl.semaphore_signal(barrier, inc=1, device_id=(r - 1, c), device_id_type=MESH)
+
+    pl.semaphore_wait(barrier, 3 + jnp.where(has_up, 1, 0) + jnp.where(has_down, 1, 0))
+
+    center = (upper_ref[0] + lower_ref[0]) * 0.5
+    half_width = (upper_ref[0] - lower_ref[0]) * 0.5
+
+    def gather(g, i):
+        slot, part, to = GATHER[i]
+        src, dst = rows.at[g, slot], rows.at[g, slot ^ to]
+        if part is not None:
+            src, dst = src.at[halves[part]], dst.at[halves[part]]
+        return send(src, dst, gather_send.at[g, i], gather_recv.at[g, i], (r, peer(to)))
+
+    def chain_up(g, q):
+        return send(cols.at[g, q], cols.at[g, q], chain_up_send.at[g, q], chain_recv.at[g, q], (r + 1, c))
+
+    def chain_down(g, q):
+        return send(cols.at[g, q], cols.at[g, q], chain_down_send.at[g, q], chain_recv.at[g, q], (r - 1, c))
+
+    def sum_up(g, s):
+        return send(up_out.at[g, s], up_in.at[g, s], up_send.at[g, s], up_recv.at[g, s], (r + 1, c))
+
+    def sum_down(g, s):
+        return send(down_out.at[g, s], down_in.at[g, s], down_send.at[g, s], down_recv.at[g, s], (r - 1, c))
+
+    def core_copy(g, j):
+        i = j // 2
+        return send(core_out.at[g, i], core_in.at[g, i], core_send.at[g, i], core_recv.at[g, i], (r, peer(1)))
+
+    def diag_copy(g, i):
+        return send(diag_out.at[g, i], diag_in.at[g, i], diag_send.at[g, i], diag_recv.at[g, i], (r, peer((2, 4)[i])))
+
+    def quad_copy(g, i, part):
+        return send(
+            quad_out.at[g, i, halves[part]], quad_in.at[g, i, halves[part]],
+            quad_send.at[g, i, part], quad_recv.at[g, i, part], (r, peer((2, 4)[i])),
+        )
+
+    def mirror_step(g, j):
+        if g == 0:
+            dense_copy(j).wait()
+        a = peer(j)
+        turned = rows[g, j].T
+
+        def one(s, carry):
+            product = jnp.dot(turned, dense[a, s], preferred_element_type=f32)
+            if j == 0:
+                mirror_t[s] = product
+            else:
+                mirror_t[s] += product
+            return carry
+
+        lax.fori_loop(0, n_row, one, 0)
+
+    def forward_step(g, q, first=False):
+        def one(a, carry):
+            product = jnp.dot(dense[a, q], cols[g, q], preferred_element_type=f32)
+            if first:
+                forward[a] = product
+            else:
+                forward[a] += product
+            return carry
+
+        lax.fori_loop(0, n_col, one, 0)
+
+    def mirror_of(s):
+        return mirror_t[s].T
+
+    def chain_arrive(g, d):
+        @pl.when(r >= d)
+        def _():
+            chain_up(g, r - d).wait_recv()
+
+            @pl.when(has_up)
+            def _():
+                chain_up(g, r - d).start()
+
+        @pl.when(r < n_row - d)
+        def _():
+            chain_down(g, r + d).wait_recv()
+
+            @pl.when(has_down)
+            def _():
+                chain_down(g, r + d).start()
+
+    def chain_use(g, d):
+        @pl.when(r >= d)
+        def _():
+            forward_step(g, r - d)
+
+        @pl.when(r < n_row - d)
+        def _():
+            forward_step(g, r + d)
+
+    def sum_hop(g, t):
+        @pl.when(has_down & has_up & (r <= t))
+        def _():
+            s = r + n_row - 1 - t
+            sum_up(g, s).wait_recv()
+            up_out[g, s] = (mirror_of(s) + up_in[g, s].astype(f32)).astype(bf16)
+            sum_up(g, s).start()
+
+        @pl.when(has_down & has_up & (n_row - 1 - r <= t))
+        def _():
+            s = t - (n_row - 1 - r)
+            sum_down(g, s).wait_recv()
+            down_out[g, s] = (mirror_of(s) + down_in[g, s].astype(f32)).astype(bf16)
+            sum_down(g, s).start()
+
+    current[...] = x_ref[...].astype(f32)
+    for g in range(DEGREE):
+        operand = current[...].astype(bf16)
+        rows[g, 0] = operand
+        cols[g, r] = operand
+
+        @pl.when(has_up)
+        def _():
+            chain_up(g, r).start()
+
+        @pl.when(has_down)
+        def _():
+            chain_down(g, r).start()
+
+        for i in (1, 2, 0):
+            gather(g, i).start()
+        mirror_step(g, 0)
+        gather(g, 0).wait_recv()
+        mirror_step(g, 1)
+        for i, onward in ((1, (3, 5)), (2, (4, 6))):
+            gather(g, i).wait_recv()
+            for k in onward:
+                gather(g, k).start()
+        chain_arrive(g, 1)
+        for i, j in ((None, 2), (None, 4), (5, 3), (6, 5)):
+            if i is not None:
+                gather(g, i).wait_recv()
+            mirror_step(g, j)
+        for i, onward in ((3, 7), (4, 8)):
+            gather(g, i).wait_recv()
+            gather(g, onward).start()
+        mirror_step(g, 6)
+        gather(g, 7).wait_recv()
+        gather(g, 8).wait_recv()
+        mirror_step(g, 7)
+
+        @pl.when(r == 0)
+        def _():
+            for s in range(n_row - 1, 0, -1):
+                up_out[g, s] = mirror_of(s).astype(bf16)
+                sum_up(g, s).start()
+
+        @pl.when(r == n_row - 1)
+        def _():
+            for s in range(n_row - 1):
+                down_out[g, s] = mirror_of(s).astype(bf16)
+                sum_down(g, s).start()
+
+        forward_step(g, r, first=True)
+        chain_use(g, 1)
+        for d in range(2, n_row):
+            chain_arrive(g, d)
+            chain_use(g, d)
+
+        for j in (7, 3, 5, 1):
+            core_out[g, j // 2] = forward[peer(j)].astype(bf16)
+            core_copy(g, j).start()
+        sum_hop(g, 1)
+
+        def paired(j):
+            return forward[peer(j)] + core_in[g, j // 2].astype(f32)
+
+        core_copy(g, 7).wait_recv()
+        total = paired(6).astype(bf16)
+        for i in (0, 1):
+            diag_out[g, i] = total[i * half:(i + 1) * half]
+            diag_copy(g, i).start()
+        for i, j, free in ((0, 2, 0), (1, 4, 1)):
+            core_copy(g, j + 1).wait_recv()
+            forward[peer(j)] = paired(j)
+            quad_out[g, i, halves[free]] = forward[peer(j), halves[free]].astype(bf16)
+            quad_copy(g, i, free).start()
+        for i, j, late, source in ((1, 4, 0, 0), (0, 2, 1, 1)):
+            diag_copy(g, source).wait_recv()
+            quad_out[g, i, halves[late]] = (
+                forward[peer(j), halves[late]] + diag_in[g, source].astype(f32)
+            ).astype(bf16)
+            quad_copy(g, i, late).start()
+
+        for t in range(2, n_row - 1):
+            sum_hop(g, t)
+        core_copy(g, 1).wait_recv()
+        forward[c] = paired(0) + mirror_of(r)
+        for i in (0, 1):
+            for part in (0, 1):
+                quad_copy(g, i, part).wait_recv()
+        forward[c] += quad_in[g, 0].astype(f32) + quad_in[g, 1].astype(f32)
+
+        @pl.when(has_down)
+        def _():
+            sum_up(g, r).wait_recv()
+            forward[c] += up_in[g, r].astype(f32)
+
+        @pl.when(has_up)
+        def _():
+            sum_down(g, r).wait_recv()
+            forward[c] += down_in[g, r].astype(f32)
+
+        shifted = forward[c] - center * current[...]
+        if g == 0:
+            following = shifted / half_width
+        else:
+            following = 2.0 * shifted / half_width - previous[...]
+        if g == DEGREE - 1:
+            out_ref[...] = following
+        else:
+            previous[...] = current[...]
+            current[...] = following
+
+    for g in range(DEGREE):
+        for i in range(len(GATHER)):
+            gather(g, i).wait_send()
+        for j in (1, 3, 5, 7):
+            core_copy(g, j).wait_send()
+        for i in (0, 1):
+            diag_copy(g, i).wait_send()
+            for part in (0, 1):
+                quad_copy(g, i, part).wait_send()
+        for q in range(n_row):
+            @pl.when(has_up & (q <= r))
+            def _():
+                chain_up(g, q).wait_send()
+
+            @pl.when(has_down & (q >= r))
+            def _():
+                chain_down(g, q).wait_send()
+
+            @pl.when(q > r)
+            def _():
+                sum_up(g, q).wait_send()
+
+            @pl.when(q < r)
+            def _():
+                sum_down(g, q).wait_send()
+
+
+def filter_call(vectors, lower_edge, upper_edge, dense, n_row, n_col):
+    seg, width = vectors.shape
+    half = seg // 2
+    f32, bf16 = jnp.float32, jnp.bfloat16
+    vmem, dma = pltpu.VMEM, pltpu.SemaphoreType.DMA
+    g = DEGREE
+    scratch = [
+        vmem(dense.shape, bf16),
+        vmem((g, n_col, seg, width), bf16),
+        vmem((g, n_row, seg, width), bf16),
+        vmem((n_row, width, seg), f32),
+        vmem((n_col, seg, width), f32),
+        vmem((seg, width), f32),
+        vmem((seg, width), f32),
+        vmem((g, n_col // 2, seg, width), bf16),
+        vmem((g, n_col // 2, seg, width), bf16),
+        vmem((g, 2, half, width), bf16),
+        vmem((g, 2, half, width), bf16),
+        vmem((g, 2, seg, width), bf16),
+        vmem((g, 2, seg, width), bf16),
+    ]
+    scratch += [vmem((g, n_row, seg, width), bf16)] * 4
+    scratch += [dma((n_col,))] + [dma((g, len(GATHER)))] * 2 + [dma((g, n_row))] * 3
+    scratch += [dma((g, n_col // 2))] * 2 + [dma((g, 2))] * 2 + [dma((g, 2, 2))] * 2
+    scratch += [dma((g, n_row))] * 4
+    return pl.pallas_call(
+        functools.partial(filter_kernel, n_row, n_col),
+        out_shape=jax.ShapeDtypeStruct((seg, width), f32),
+        in_specs=[
+            pl.BlockSpec(memory_space=pltpu.VMEM),
+            pl.BlockSpec(memory_space=pltpu.SMEM),
+            pl.BlockSpec(memory_space=pltpu.SMEM),
+            pl.BlockSpec(memory_space=pl.ANY),
+        ],
+        out_specs=pl.BlockSpec(memory_space=pltpu.VMEM),
+        scratch_shapes=scratch,
+        compiler_params=pltpu.CompilerParams(
+            collective_id=0, has_side_effects=True, vmem_limit_bytes=56 * 2**20
+        ),
+        name="filter",
+    )(vectors, lower_edge, upper_edge, dense)
+
+
+def per_device_dense(
+    n_row, n_col, vectors, blocks, block_rows, block_cols, block_count, lower_edge, upper_edge
+):
+    dense = densify(
+        blocks[0, 0], block_rows[0, 0], block_cols[0, 0], block_count, n_row, n_col, vectors.shape[0]
+    )
+    return filter_call(vectors, lower_edge, upper_edge, dense, n_row, n_col)
+
+
+def per_device_any(n_row, n_col, vectors, *others):
+    dense_bytes = 2 * n_row * n_col * vectors.shape[0] ** 2
+    if n_col == 8 and n_row >= 2 and dense_bytes <= 16 * 2**20:
+        return per_device_dense(n_row, n_col, vectors, *others)
+    return per_device(vectors, *others)
+
+
 def solution(mesh):
     return jax.shard_map(
-        per_device,
+        functools.partial(per_device_any, mesh.shape["row"], mesh.shape["col"]),
         mesh=mesh,
         in_specs=(
             P(("row", "col"), None),

time: 740 us -> 123 us (0.17); the launches traced: 725 us -> 122 us
  matrix products: 372 us -> 0 us
  waiting for transfers between devices: 301 us -> 0 us
  Pallas kernels: 0 us -> 116 us
  local copies, waits for them, and re-layouts: 25.5 us -> 3.22 us
  between operations: 15.3 us -> 1.96 us
  other arithmetic: 9.4 us -> 0 us
    dot_general x64 -> x0, matrix products: 372 us -> none  [the longest x16 111 us: place_sum(): jnp.einsum('gt,giv->tiv', table, upper, preferred_element_type=jnp.float32)]
    reduce_scatter x4 -> x0, waiting for transfers between devices: 182 us -> none  [the longest x2 109 us: per_device(): forward = lax.psum_scatter(row_part, 'col', scatter_dimension=0, tiled=True)]
    all_gather x4 -> x0, waiting for transfers between devices: 117 us -> none  [the longest x2 58.9 us: per_device(): cols_side = lax.all_gather(operand, 'row', axis=0, tiled=True)]
    pallas_call x0 -> x2, Pallas kernels: none -> 116 us  [the longest x1 100 us: filter_call(): pl.pallas_call(functools.partial(filter_kernel, n_row, n_col), out_shape=...]
    while x60 -> x0, local copies, waits for them, and re-layouts: 21.6 us -> none  [the longest x4 21.5 us: slot_products(): lax.fori_loop(0, group_limit, group_step, start_totals)]
  transfers between devices with their start and end apart: 8 -> 0, of which waited for: 8 -> 0; matrix products, arithmetic and copies ran while one was open for 2% -> 0% of each run, Pallas kernels for 0% -> 0%
where the time goes in v1:
time: 123 us; the launch traced here: 122 us
  Pallas kernels  116 us (94%)
  local copies, waits for them, and re-layouts  3.22 us (3%)
  between operations  1.96 us (2%)
    pallas_call x1, Pallas kernels, filter_call(): pl.pallas_call(functools.partial(filter_kernel, n_row, n_col), out_shape=...  100 us
    pallas_call x1, Pallas kernels, densify(): pl.pallas_call(densify_kernel, out_shape=jax.ShapeDtypeStruct((col_segs,...  16.1 us
    unnamed x5, local copies, waits for them, and re-layouts  3.22 us

profile of v1, /device:TPU:0, one launch (start us, length us, event | category | flops | bytes accessed | tf_op | source)
XLA Modules:
  0.0 121.5 jit_solution(11964470050866389187)
XLA Ops:
  1.9 0.0 copy-start
  2.0 0.7 copy-done
  2.6 0.0 copy-start.1
  2.6 0.7 copy-done.1
  3.3 16.1 %densify.1.dense_hbm = bf16[8,4,512,512]{3,2,1,0:T(8,128)(2,1)} custom-call(s32[256]{0:T(256)S(1)} %bitcast.3, s32[256]{0:T(256)S(1)} %bitcast.4, s32[1,1]{1,0:T(1,128)S(6)} %copy.9.count_ref, bf16[256,128,128]{2,1,0:T(8,128)(2,1)} %bitcast.5), custom_call_target="tpu_custom_call" | custom-call | tf_op jit(solution)/shard_map/densify/pallas_call | solution.py:174
  19.4 100.2 %filter.1 = f32[512,256]{1,0:T(8,128)} custom-call(bf16[512,256]{1,0:T(8,128)(2,1)} %x_ref.1, f32[1]{0:T(128)S(6)} %copy.10.lower_ref, f32[1]{0:T(128)S(6)} %copy.11.upper_ref, bf16[8,4,512,512]{3,2,1,0:T(8,128)(2,1)} %densify.1.dense_hbm), custom_call_target="tpu_custom_call" | custom-call | tf_op jit(solution)/shard_map/filter/pallas_call | solution.py:510
  119.7 1.9 %copy.12 = f32[512,256]{1,0:T(8,128)} copy(f32[512,256]{1,0:T(8,128)} %filter.1) | data formatting | bytes 1048576
Async XLA Ops:
  1.9 0.7 copy-start
  2.6 0.7 copy-start.1

commit v2 on v1

--- a/solution.py
+++ b/solution.py
@@ -108,77 +108,73 @@
     return current
 
 
-def densify_kernel(rows_ref, cols_ref, count_ref, blocks_ref, dense_ref, head, follow):
-    col_segs, row_segs, seg, _ = dense_ref.shape
-    block = blocks_ref.shape[1]
-    per_seg = seg // block
-    col_blocks = row_segs * per_seg
+def link_kernel(
+    col_blocks, rows_ref, cols_ref, count_ref, blocks_hbm, table_ref, sums_ref, held, follow, repeats, sem
+):
+    slots = blocks_hbm.shape[2]
+    empty = follow.shape[0] - 1
     count = count_ref[0, 0]
-
-    def clear_head(i, carry):
-        head[i] = -1
+    load = pltpu.make_async_copy(blocks_hbm.at[0, 0], held, sem)
+    load.start()
+
+    def clear(i, carry):
+        for k in range(16):
+            table_ref[i * 16 + k] = empty
         return carry
 
-    lax.fori_loop(0, head.shape[0], clear_head, 0, unroll=8)
-
-    def link(i, carry):
-        slot = count - 1 - i
-        place = rows_ref[slot] * col_blocks + cols_ref[slot]
-        follow[slot] = head[place]
-        head[place] = slot
+    lax.fori_loop(0, table_ref.shape[0] // 16, clear, 0)
+    follow[empty] = -1
+
+    def link(slot, found):
+        place = rows_ref[0, 0, slot] * col_blocks + cols_ref[0, 0, slot]
+        before = table_ref[place]
+        follow[slot] = before
+        table_ref[place] = slot
+        repeats[found] = place
+        return found + jnp.where(follow[before] == empty, 1, 0)
+
+    found = lax.fori_loop(0, count, link, 0)
+    load.wait()
+
+    def sum_place(i, carry):
+        place = repeats[i]
+        last = table_ref[place]
+
+        def more(state):
+            return state[0] != empty
+
+        def add(state):
+            at, total = state
+            return follow[at], total + held[at].astype(jnp.float32)
+
+        _, total = lax.while_loop(more, add, (follow[last], held[last].astype(jnp.float32)))
+        sums_ref[i] = total.astype(sums_ref.dtype)
+        table_ref[place] = slots + i
         return carry
 
-    lax.fori_loop(0, count, link, 0)
-
-    def clear(i, carry):
-        dense_ref[i // row_segs, i % row_segs] = jnp.zeros((seg, seg), dense_ref.dtype)
-        return carry
-
-    lax.fori_loop(0, col_segs * row_segs, clear, 0)
-
-    def place_slot(slot, carry):
-        row, col = rows_ref[slot], cols_ref[slot]
-        after = follow[slot]
-        is_first = head[row * col_blocks + col] == slot
-        target = dense_ref.at[
-            row // per_seg,
-            col // per_seg,
-            pl.ds(pl.multiple_of((row % per_seg) * block, block), block),
-            pl.ds(pl.multiple_of((col % per_seg) * block, block), block),
-        ]
-
-        @pl.when(is_first & (after < 0))
-        def _():
-            target[...] = blocks_ref[slot]
-
-        @pl.when(is_first & (after >= 0))
-        def _():
-            def more(state):
-                return state[0] >= 0
-
-            def add(state):
-                at, total = state
-                return follow[at], total + blocks_ref[at].astype(jnp.float32)
-
-            _, total = lax.while_loop(more, add, (after, blocks_ref[slot].astype(jnp.float32)))
-            target[...] = total.astype(dense_ref.dtype)
-
-        return carry
-
-    lax.fori_loop(0, count, place_slot, 0)
-
-
-def densify(blocks, block_rows, block_cols, block_count, row_segs, col_segs, seg):
-    slots, block, _ = blocks.shape
-    places = col_segs * row_segs * (seg // block) ** 2
+    lax.fori_loop(0, found, sum_place, 0)
+
+
+def link_call(blocks, block_rows, block_cols, block_count, row_blocks, col_blocks):
+    _, _, slots, block, _ = blocks.shape
+    sums = slots // 2
+    smem = pl.BlockSpec(memory_space=pltpu.SMEM)
     return pl.pallas_call(
-        densify_kernel,
-        out_shape=jax.ShapeDtypeStruct((col_segs, row_segs, seg, seg), jnp.bfloat16),
-        in_specs=[pl.BlockSpec(memory_space=pltpu.SMEM)] * 3 + [pl.BlockSpec(memory_space=pltpu.VMEM)],
-        out_specs=pl.BlockSpec(memory_space=pltpu.VMEM),
-        scratch_shapes=[pltpu.SMEM((places,), jnp.int32), pltpu.SMEM((slots,), jnp.int32)],
-        compiler_params=pltpu.CompilerParams(vmem_limit_bytes=48 * 2**20),
-        name="densify",
+        functools.partial(link_kernel, col_blocks),
+        out_shape=(
+            jax.ShapeDtypeStruct((row_blocks * col_blocks,), jnp.int32),
+            jax.ShapeDtypeStruct((sums, block, block), jnp.bfloat16),
+        ),
+        in_specs=[smem] * 3 + [pl.BlockSpec(memory_space=pl.ANY)],
+        out_specs=(smem, pl.BlockSpec(memory_space=pltpu.VMEM)),
+        scratch_shapes=[
+            pltpu.VMEM((slots, block, block), jnp.bfloat16),
+            pltpu.SMEM((slots + sums + 1,), jnp.int32),
+            pltpu.SMEM((slots + 1,), jnp.int32),
+            pltpu.SemaphoreType.DMA,
+        ],
+        compiler_params=pltpu.CompilerParams(vmem_limit_bytes=62 * 2**20),
+        name="link",
     )(block_rows, block_cols, block_count, blocks)
 
 
@@ -191,11 +187,11 @@
 
 
 def filter_kernel(
-    n_row, n_col, x_ref, lower_ref, upper_ref, dense_hbm, out_ref,
-    dense, rows, cols, mirror_t, forward, current, previous,
+    n_row, n_col, x_ref, lower_ref, upper_ref, table_ref, blocks_hbm, sums_hbm, out_ref,
+    pool, dense, rows, cols, mirror_t, forward, current, previous,
     core_out, core_in, diag_out, diag_in, quad_out, quad_in,
     up_out, up_in, down_out, down_in,
-    dense_sem, gather_send, gather_recv, chain_up_send, chain_down_send, chain_recv,
+    pool_sem, gather_send, gather_recv, chain_up_send, chain_down_send, chain_recv,
     core_send, core_recv, diag_send, diag_recv, quad_send, quad_recv,
     up_send, up_recv, down_send, down_recv,
 ):
@@ -220,11 +216,14 @@
             device_id=device, device_id_type=MESH,
         )
 
-    def dense_copy(j):
-        return pltpu.make_async_copy(dense_hbm.at[peer(j)], dense.at[peer(j)], dense_sem.at[j])
-
-    for j in range(n_col):
-        dense_copy(j).start()
+    slots, sums = blocks_hbm.shape[2], sums_hbm.shape[0]
+    loads = (
+        pltpu.make_async_copy(blocks_hbm.at[0, 0], pool.at[pl.ds(0, slots)], pool_sem.at[0]),
+        pltpu.make_async_copy(sums_hbm, pool.at[pl.ds(slots, sums)], pool_sem.at[1]),
+    )
+    for load in loads:
+        load.start()
+    pool[slots + sums] = jnp.zeros(pool.shape[1:], pool.dtype)
 
     barrier = pltpu.get_barrier_semaphore()
     for j in (1, 2, 4):
@@ -275,10 +274,25 @@
             quad_send.at[g, i, part], quad_recv.at[g, i, part], (r, peer((2, 4)[i])),
         )
 
+    block = pool.shape[1]
+    per_seg = seg // block
+
+    def assemble(a):
+        def one(i, carry):
+            row, s = i // n_row, i % n_row
+            first = ((a * per_seg + row) * n_row + s) * per_seg
+            for k in range(per_seg):
+                dense[
+                    a, s, pl.ds(pl.multiple_of(row * block, block), block), pl.ds(k * block, block)
+                ] = pool[table_ref[first + k]]
+            return carry
+
+        lax.fori_loop(0, per_seg * n_row, one, 0)
+
     def mirror_step(g, j):
+        a = peer(j)
         if g == 0:
-            dense_copy(j).wait()
-        a = peer(j)
+            assemble(a)
         turned = rows[g, j].T
 
         def one(s, carry):
@@ -302,6 +316,12 @@
 
         lax.fori_loop(0, n_col, one, 0)
 
+    q_last = jnp.where(2 * r < n_row, n_row - 1, 0)
+
+    def forward_last(g, j):
+        a = peer(j)
+        forward[a] += jnp.dot(dense[a, q_last], cols[g, q_last], preferred_element_type=f32)
+
     def mirror_of(s):
         return mirror_t[s].T
 
@@ -323,11 +343,11 @@
                 chain_down(g, r + d).start()
 
     def chain_use(g, d):
-        @pl.when(r >= d)
+        @pl.when((r >= d) & (r - d != q_last))
         def _():
             forward_step(g, r - d)
 
-        @pl.when(r < n_row - d)
+        @pl.when((r < n_row - d) & (r + d != q_last))
         def _():
             forward_step(g, r + d)
 
@@ -362,6 +382,9 @@
 
         for i in (1, 2, 0):
             gather(g, i).start()
+        if g == 0:
+            for load in loads:
+                load.wait()
         mirror_step(g, 0)
         gather(g, 0).wait_recv()
         mirror_step(g, 1)
@@ -378,6 +401,8 @@
             gather(g, i).wait_recv()
             gather(g, onward).start()
         mirror_step(g, 6)
+        if n_row > 2:
+            chain_arrive(g, 2)
         gather(g, 7).wait_recv()
         gather(g, 8).wait_recv()
         mirror_step(g, 7)
@@ -397,13 +422,16 @@
         forward_step(g, r, first=True)
         chain_use(g, 1)
         for d in range(2, n_row):
-            chain_arrive(g, d)
+            if d > 2:
+                chain_arrive(g, d)
             chain_use(g, d)
 
         for j in (7, 3, 5, 1):
+            forward_last(g, j)
             core_out[g, j // 2] = forward[peer(j)].astype(bf16)
             core_copy(g, j).start()
-        sum_hop(g, 1)
+        for j in (6, 2, 4, 0):
+            forward_last(g, j)
 
         def paired(j):
             return forward[peer(j)] + core_in[g, j // 2].astype(f32)
@@ -418,6 +446,7 @@
             forward[peer(j)] = paired(j)
             quad_out[g, i, halves[free]] = forward[peer(j), halves[free]].astype(bf16)
             quad_copy(g, i, free).start()
+        sum_hop(g, 1)
         for i, j, late, source in ((1, 4, 0, 0), (0, 2, 1, 1)):
             diag_copy(g, source).wait_recv()
             quad_out[g, i, halves[late]] = (
@@ -482,14 +511,15 @@
                 sum_down(g, q).wait_send()
 
 
-def filter_call(vectors, lower_edge, upper_edge, dense, n_row, n_col):
+def filter_call(vectors, lower_edge, upper_edge, table, blocks, sums, n_row, n_col):
     seg, width = vectors.shape
     half = seg // 2
     f32, bf16 = jnp.float32, jnp.bfloat16
     vmem, dma = pltpu.VMEM, pltpu.SemaphoreType.DMA
     g = DEGREE
     scratch = [
-        vmem(dense.shape, bf16),
+        vmem((blocks.shape[2] + sums.shape[0] + 1,) + sums.shape[1:], bf16),
+        vmem((n_col, n_row, seg, seg), bf16),
         vmem((g, n_col, seg, width), bf16),
         vmem((g, n_row, seg, width), bf16),
         vmem((n_row, width, seg), f32),
@@ -504,7 +534,7 @@
         vmem((g, 2, seg, width), bf16),
     ]
     scratch += [vmem((g, n_row, seg, width), bf16)] * 4
-    scratch += [dma((n_col,))] + [dma((g, len(GATHER)))] * 2 + [dma((g, n_row))] * 3
+    scratch += [dma((2,))] + [dma((g, len(GATHER)))] * 2 + [dma((g, n_row))] * 3
     scratch += [dma((g, n_col // 2))] * 2 + [dma((g, 2))] * 2 + [dma((g, 2, 2))] * 2
     scratch += [dma((g, n_row))] * 4
     return pl.pallas_call(
@@ -514,24 +544,27 @@
             pl.BlockSpec(memory_space=pltpu.VMEM),
             pl.BlockSpec(memory_space=pltpu.SMEM),
             pl.BlockSpec(memory_space=pltpu.SMEM),
+            pl.BlockSpec(memory_space=pltpu.SMEM),
+            pl.BlockSpec(memory_space=pl.ANY),
             pl.BlockSpec(memory_space=pl.ANY),
         ],
         out_specs=pl.BlockSpec(memory_space=pltpu.VMEM),
         scratch_shapes=scratch,
         compiler_params=pltpu.CompilerParams(
-            collective_id=0, has_side_effects=True, vmem_limit_bytes=56 * 2**20
+            collective_id=0, has_side_effects=True, vmem_limit_bytes=62 * 2**20
         ),
         name="filter",
-    )(vectors, lower_edge, upper_edge, dense)
+    )(vectors, lower_edge, upper_edge, table, blocks, sums)
 
 
 def per_device_dense(
     n_row, n_col, vectors, blocks, block_rows, block_cols, block_count, lower_edge, upper_edge
 ):
-    dense = densify(
-        blocks[0, 0], block_rows[0, 0], block_cols[0, 0], block_count, n_row, n_col, vectors.shape[0]
+    per_seg = vectors.shape[0] // blocks.shape[-1]
+    table, sums = link_call(
+        blocks, block_rows, block_cols, block_count, n_col * per_seg, n_row * per_seg
     )
-    return filter_call(vectors, lower_edge, upper_edge, dense, n_row, n_col)
+    return filter_call(vectors, lower_edge, upper_edge, table, blocks, sums, n_row, n_col)
 
 
 def per_device_any(n_row, n_col, vectors, *others):

time: 123 us -> 102 us (0.83)
  Pallas kernels: 116 us -> 97.4 us
  local copies, waits for them, and re-layouts: 3.22 us -> 1.87 us
    pallas_call x1, Pallas kernels: 16.1 us -> 6.42 us  [link_call(): pl.pallas_call(functools.partial(link_kernel, col_blocks), out_shape=(jax...]
    pallas_call x1, Pallas kernels: 100 us -> 91 us  [filter_call(): pl.pallas_call(functools.partial(filter_kernel, n_row, n_col), out_shape=...]
    unnamed x5 -> x1, local copies, waits for them, and re-layouts: 3.22 us -> 1.87 us
where the time goes in v2:
time: 102 us; the launch traced here: 101 us
  Pallas kernels  97.4 us (95%)
  between operations  1.96 us (2%)
  local copies, waits for them, and re-layouts  1.87 us (2%)
    pallas_call x1, Pallas kernels, filter_call(): pl.pallas_call(functools.partial(filter_kernel, n_row, n_col), out_shape=...  91 us
    pallas_call x1, Pallas kernels, link_call(): pl.pallas_call(functools.partial(link_kernel, col_blocks), out_shape=(jax...  6.42 us

profile of v2, /device:TPU:0, one launch (start us, length us, event | category | flops | bytes accessed | tf_op | source)
XLA Modules:
  0.0 101.3 jit_solution(12909564234386663316)
XLA Ops:
  1.9 6.4 %link.1 = (s32[512]{0:T(512)}, bf16[128,128,128]{2,1,0:T(8,128)(2,1)}) custom-call(s32[1,1,256]{2,1,0:T(1,128)} %rows_ref.1, s32[1,1,256]{2,1,0:T(1,128)} %cols_ref.1, s32[1,1]{1,0:T(1,128)S(6)} %copy.9.count_ref, bf16[1,1,256,128,128]{4,3,2,1,0:T(8,128)(2,1)} %blocks_hbm.3), custom_call_target="tpu_custom_call" | custom-call | tf_op jit(solution)/shard_map/link/pallas_call | solution.py:162
  8.4 91.0 %filter.1 = f32[512,256]{1,0:T(8,128)} custom-call(bf16[512,256]{1,0:T(8,128)(2,1)} %x_ref.1, f32[1]{0:T(128)S(6)} %copy.10.lower_ref, f32[1]{0:T(128)S(6)} %copy.11.upper_ref, s32[512]{0:T(512)} %get-tuple-element.7.table_ref, bf16[1,1,256,128,128]{4,3,2,1,0:T(8,128)(2,1)} %blocks_hbm.3, bf16[128,128,128]{2,1,0:T(8,128)(2,1)} %get-tuple-element.8.sums_hbm), custom_call_target="tpu_custom_call" | custom-call | tf_op jit(solution)/shard_map/filter/pallas_call | solution.py:540
  99.4 1.9 %copy.12 = f32[512,256]{1,0:T(8,128)} copy(f32[512,256]{1,0:T(8,128)} %filter.1) | data formatting | bytes 1048576

commit v3 on v2

--- a/solution.py
+++ b/solution.py
@@ -179,7 +179,7 @@
 
 
 GATHER = (
-    (0, None, 1), (0, None, 2), (0, None, 4),
+    (0, None, 1), (0, 0, 2), (0, 1, 4), (0, 1, 2), (0, 0, 4),
     (2, 0, 4), (4, 1, 2),
     (2, None, 1), (4, None, 1),
     (6, 0, 1), (6, 1, 1),
@@ -249,17 +249,25 @@
             src, dst = src.at[halves[part]], dst.at[halves[part]]
         return send(src, dst, gather_send.at[g, i], gather_recv.at[g, i], (r, peer(to)))
 
-    def chain_up(g, q):
-        return send(cols.at[g, q], cols.at[g, q], chain_up_send.at[g, q], chain_recv.at[g, q], (r + 1, c))
-
-    def chain_down(g, q):
-        return send(cols.at[g, q], cols.at[g, q], chain_down_send.at[g, q], chain_recv.at[g, q], (r - 1, c))
-
-    def sum_up(g, s):
-        return send(up_out.at[g, s], up_in.at[g, s], up_send.at[g, s], up_recv.at[g, s], (r + 1, c))
-
-    def sum_down(g, s):
-        return send(down_out.at[g, s], down_in.at[g, s], down_send.at[g, s], down_recv.at[g, s], (r - 1, c))
+    def chain_up(g, q, p):
+        part = cols.at[g, q, halves[p]]
+        return send(part, part, chain_up_send.at[g, q, p], chain_recv.at[g, q, p], (r + 1, c))
+
+    def chain_down(g, q, p):
+        part = cols.at[g, q, halves[p]]
+        return send(part, part, chain_down_send.at[g, q, p], chain_recv.at[g, q, p], (r - 1, c))
+
+    def sum_up(g, s, p):
+        return send(
+            up_out.at[g, s, halves[p]], up_in.at[g, s, halves[p]],
+            up_send.at[g, s, p], up_recv.at[g, s, p], (r + 1, c),
+        )
+
+    def sum_down(g, s, p):
+        return send(
+            down_out.at[g, s, halves[p]], down_in.at[g, s, halves[p]],
+            down_send.at[g, s, p], down_recv.at[g, s, p], (r - 1, c),
+        )
 
     def core_copy(g, j):
         i = j // 2
@@ -322,25 +330,48 @@
         a = peer(j)
         forward[a] += jnp.dot(dense[a, q_last], cols[g, q_last], preferred_element_type=f32)
 
-    def mirror_of(s):
-        return mirror_t[s].T
-
-    def chain_arrive(g, d):
+    def mirror_of(s, p):
+        return mirror_t[s, :, halves[p]].T
+
+    def mirror_last(g, j):
+        a = peer(j)
+        if g == 0:
+            assemble(a)
+        turned = rows[g, j].T
+        for i in range(n_row):
+            s = jnp.where(2 * r < n_row, n_row - 1 - i, i)
+            mirror_t[s] += jnp.dot(turned, dense[a, s], preferred_element_type=f32)
+            if i == n_row - 1:
+                break
+
+            @pl.when(r == 0)
+            def _():
+                for p in (0, 1):
+                    up_out[g, n_row - 1 - i, halves[p]] = mirror_of(n_row - 1 - i, p).astype(bf16)
+                    sum_up(g, n_row - 1 - i, p).start()
+
+            @pl.when(r == n_row - 1)
+            def _():
+                for p in (0, 1):
+                    down_out[g, i, halves[p]] = mirror_of(i, p).astype(bf16)
+                    sum_down(g, i, p).start()
+
+    def chain_arrive(g, d, p):
         @pl.when(r >= d)
         def _():
-            chain_up(g, r - d).wait_recv()
+            chain_up(g, r - d, p).wait_recv()
 
             @pl.when(has_up)
             def _():
-                chain_up(g, r - d).start()
+                chain_up(g, r - d, p).start()
 
         @pl.when(r < n_row - d)
         def _():
-            chain_down(g, r + d).wait_recv()
+            chain_down(g, r + d, p).wait_recv()
 
             @pl.when(has_down)
             def _():
-                chain_down(g, r + d).start()
+                chain_down(g, r + d, p).start()
 
     def chain_use(g, d):
         @pl.when((r >= d) & (r - d != q_last))
@@ -351,20 +382,20 @@
         def _():
             forward_step(g, r + d)
 
-    def sum_hop(g, t):
+    def sum_hop(g, t, p):
         @pl.when(has_down & has_up & (r <= t))
         def _():
             s = r + n_row - 1 - t
-            sum_up(g, s).wait_recv()
-            up_out[g, s] = (mirror_of(s) + up_in[g, s].astype(f32)).astype(bf16)
-            sum_up(g, s).start()
+            sum_up(g, s, p).wait_recv()
+            up_out[g, s, halves[p]] = (mirror_of(s, p) + up_in[g, s, halves[p]].astype(f32)).astype(bf16)
+            sum_up(g, s, p).start()
 
         @pl.when(has_down & has_up & (n_row - 1 - r <= t))
         def _():
             s = t - (n_row - 1 - r)
-            sum_down(g, s).wait_recv()
-            down_out[g, s] = (mirror_of(s) + down_in[g, s].astype(f32)).astype(bf16)
-            sum_down(g, s).start()
+            sum_down(g, s, p).wait_recv()
+            down_out[g, s, halves[p]] = (mirror_of(s, p) + down_in[g, s, halves[p]].astype(f32)).astype(bf16)
+            sum_down(g, s, p).start()
 
     current[...] = x_ref[...].astype(f32)
     for g in range(DEGREE):
@@ -374,13 +405,15 @@
 
         @pl.when(has_up)
         def _():
-            chain_up(g, r).start()
+            for p in (0, 1):
+                chain_up(g, r, p).start()
 
         @pl.when(has_down)
         def _():
-            chain_down(g, r).start()
-
-        for i in (1, 2, 0):
+            for p in (0, 1):
+                chain_down(g, r, p).start()
+
+        for i in (1, 2, 3, 4, 0):
             gather(g, i).start()
         if g == 0:
             for load in loads:
@@ -388,42 +421,39 @@
         mirror_step(g, 0)
         gather(g, 0).wait_recv()
         mirror_step(g, 1)
-        for i, onward in ((1, (3, 5)), (2, (4, 6))):
+        for i, onward in ((1, 5), (2, 6)):
             gather(g, i).wait_recv()
-            for k in onward:
-                gather(g, k).start()
-        chain_arrive(g, 1)
-        for i, j in ((None, 2), (None, 4), (5, 3), (6, 5)):
-            if i is not None:
-                gather(g, i).wait_recv()
-            mirror_step(g, j)
+            gather(g, onward).start()
+        chain_arrive(g, 1, 0)
+        if g > 0:
+            forward_step(g, r, first=True)
         for i, onward in ((3, 7), (4, 8)):
             gather(g, i).wait_recv()
             gather(g, onward).start()
+        chain_arrive(g, 1, 1)
+        mirror_step(g, 2)
+        mirror_step(g, 4)
+        for i, onward in ((5, 9), (6, 10)):
+            gather(g, i).wait_recv()
+            gather(g, onward).start()
+        if n_row > 2:
+            chain_arrive(g, 2, 0)
+        for i, j in ((7, 3), (8, 5)):
+            gather(g, i).wait_recv()
+            mirror_step(g, j)
         mirror_step(g, 6)
         if n_row > 2:
-            chain_arrive(g, 2)
-        gather(g, 7).wait_recv()
-        gather(g, 8).wait_recv()
-        mirror_step(g, 7)
-
-        @pl.when(r == 0)
-        def _():
-            for s in range(n_row - 1, 0, -1):
-                up_out[g, s] = mirror_of(s).astype(bf16)
-                sum_up(g, s).start()
-
-        @pl.when(r == n_row - 1)
-        def _():
-            for s in range(n_row - 1):
-                down_out[g, s] = mirror_of(s).astype(bf16)
-                sum_down(g, s).start()
-
-        forward_step(g, r, first=True)
+            chain_arrive(g, 2, 1)
+        gather(g, 9).wait_recv()
+        gather(g, 10).wait_recv()
+        mirror_last(g, 7)
+        if g == 0:
+            forward_step(g, r, first=True)
         chain_use(g, 1)
         for d in range(2, n_row):
             if d > 2:
-                chain_arrive(g, d)
+                for p in (0, 1):
+                    chain_arrive(g, d, p)
             chain_use(g, d)
 
         for j in (7, 3, 5, 1):
@@ -432,6 +462,8 @@
             core_copy(g, j).start()
         for j in (6, 2, 4, 0):
             forward_last(g, j)
+        if n_row > 2:
+            sum_hop(g, 1, 0)
 
         def paired(j):
             return forward[peer(j)] + core_in[g, j // 2].astype(f32)
@@ -446,7 +478,8 @@
             forward[peer(j)] = paired(j)
             quad_out[g, i, halves[free]] = forward[peer(j), halves[free]].astype(bf16)
             quad_copy(g, i, free).start()
-        sum_hop(g, 1)
+        if n_row > 2:
+            sum_hop(g, 1, 1)
         for i, j, late, source in ((1, 4, 0, 0), (0, 2, 1, 1)):
             diag_copy(g, source).wait_recv()
             quad_out[g, i, halves[late]] = (
@@ -455,9 +488,12 @@
             quad_copy(g, i, late).start()
 
         for t in range(2, n_row - 1):
-            sum_hop(g, t)
+            for p in (0, 1):
+                sum_hop(g, t, p)
         core_copy(g, 1).wait_recv()
-        forward[c] = paired(0) + mirror_of(r)
+        forward[c] = paired(0)
+        for p in (0, 1):
+            forward[c, halves[p]] += mirror_of(r, p)
         for i in (0, 1):
             for part in (0, 1):
                 quad_copy(g, i, part).wait_recv()
@@ -465,13 +501,15 @@
 
         @pl.when(has_down)
         def _():
-            sum_up(g, r).wait_recv()
-            forward[c] += up_in[g, r].astype(f32)
+            for p in (0, 1):
+                sum_up(g, r, p).wait_recv()
+                forward[c, halves[p]] += up_in[g, r, halves[p]].astype(f32)
 
         @pl.when(has_up)
         def _():
-            sum_down(g, r).wait_recv()
-            forward[c] += down_in[g, r].astype(f32)
+            for p in (0, 1):
+                sum_down(g, r, p).wait_recv()
+                forward[c, halves[p]] += down_in[g, r, halves[p]].astype(f32)
 
         shifted = forward[c] - center * current[...]
         if g == 0:
@@ -496,19 +534,23 @@
         for q in range(n_row):
             @pl.when(has_up & (q <= r))
             def _():
-                chain_up(g, q).wait_send()
+                for p in (0, 1):
+                    chain_up(g, q, p).wait_send()
 
             @pl.when(has_down & (q >= r))
             def _():
-                chain_down(g, q).wait_send()
+                for p in (0, 1):
+                    chain_down(g, q, p).wait_send()
 
             @pl.when(q > r)
             def _():
-                sum_up(g, q).wait_send()
+                for p in (0, 1):
+                    sum_up(g, q, p).wait_send()
 
             @pl.when(q < r)
             def _():
-                sum_down(g, q).wait_send()
+                for p in (0, 1):
+                    sum_down(g, q, p).wait_send()
 
 
 def filter_call(vectors, lower_edge, upper_edge, table, blocks, sums, n_row, n_col):
@@ -534,9 +576,9 @@
         vmem((g, 2, seg, width), bf16),
     ]
     scratch += [vmem((g, n_row, seg, width), bf16)] * 4
-    scratch += [dma((2,))] + [dma((g, len(GATHER)))] * 2 + [dma((g, n_row))] * 3
+    scratch += [dma((2,))] + [dma((g, len(GATHER)))] * 2 + [dma((g, n_row, 2))] * 3
     scratch += [dma((g, n_col // 2))] * 2 + [dma((g, 2))] * 2 + [dma((g, 2, 2))] * 2
-    scratch += [dma((g, n_row))] * 4
+    scratch += [dma((g, n_row, 2))] * 4
     return pl.pallas_call(
         functools.partial(filter_kernel, n_row, n_col),
         out_shape=jax.ShapeDtypeStruct((seg, width), f32),

time: 102 us -> 97.7 us (0.958)
  Pallas kernels: 97.4 us -> 93.5 us
    pallas_call x1, Pallas kernels: 91 us -> 87.2 us  [filter_call(): pl.pallas_call(functools.partial(filter_kernel, n_row, n_col), out_shape=...]
where the time goes in v3:
time: 97.7 us; the launch traced here: 97.3 us
  Pallas kernels  93.5 us (96%)
  between operations  1.96 us (2%)
  local copies, waits for them, and re-layouts  1.87 us (2%)
    pallas_call x1, Pallas kernels, filter_call(): pl.pallas_call(functools.partial(filter_kernel, n_row, n_col), out_shape=...  87.2 us
    pallas_call x1, Pallas kernels, link_call(): pl.pallas_call(functools.partial(link_kernel, col_blocks), out_shape=(jax...  6.37 us

profile of v3, /device:TPU:0, one launch (start us, length us, event | category | flops | bytes accessed | tf_op | source)
XLA Modules:
  0.0 97.3 jit_solution(3758502411335134022)
XLA Ops:
  1.9 6.4 %link.1 = (s32[512]{0:T(512)}, bf16[128,128,128]{2,1,0:T(8,128)(2,1)}) custom-call(s32[1,1,256]{2,1,0:T(1,128)} %rows_ref.1, s32[1,1,256]{2,1,0:T(1,128)} %cols_ref.1, s32[1,1]{1,0:T(1,128)S(6)} %copy.9.count_ref, bf16[1,1,256,128,128]{4,3,2,1,0:T(8,128)(2,1)} %blocks_hbm.3), custom_call_target="tpu_custom_call" | custom-call | tf_op jit(solution)/shard_map/link/pallas_call | solution.py:162
  8.3 87.2 %filter.1 = f32[512,256]{1,0:T(8,128)} custom-call(bf16[512,256]{1,0:T(8,128)(2,1)} %x_ref.1, f32[1]{0:T(128)S(6)} %copy.10.lower_ref, f32[1]{0:T(128)S(6)} %copy.11.upper_ref, s32[512]{0:T(512)} %get-tuple-element.7.table_ref, bf16[1,1,256,128,128]{4,3,2,1,0:T(8,128)(2,1)} %blocks_hbm.3, bf16[128,128,128]{2,1,0:T(8,128)(2,1)} %get-tuple-element.8.sums_hbm), custom_call_target="tpu_custom_call" | custom-call | tf_op jit(solution)/shard_map/filter/pallas_call | solution.py:582
  95.5 1.9 %copy.12 = f32[512,256]{1,0:T(8,128)} copy(f32[512,256]{1,0:T(8,128)} %filter.1) | data formatting | bytes 1048576

commit v4 on v3

--- a/solution.py
+++ b/solution.py
@@ -297,15 +297,18 @@
 
         lax.fori_loop(0, per_seg * n_row, one, 0)
 
-    def mirror_step(g, j):
-        a = peer(j)
+    def mirror_step(g, *slots_here):
+        segments = [peer(j) for j in slots_here]
         if g == 0:
-            assemble(a)
-        turned = rows[g, j].T
+            for a in segments:
+                assemble(a)
+        turned = [rows[g, j].T for j in slots_here]
 
         def one(s, carry):
-            product = jnp.dot(turned, dense[a, s], preferred_element_type=f32)
-            if j == 0:
+            product = sum(
+                jnp.dot(t, dense[a, s], preferred_element_type=f32) for t, a in zip(turned, segments)
+            )
+            if 0 in slots_here:
                 mirror_t[s] = product
             else:
                 mirror_t[s] += product
@@ -397,50 +400,52 @@
             down_out[g, s, halves[p]] = (mirror_of(s, p) + down_in[g, s, halves[p]].astype(f32)).astype(bf16)
             sum_down(g, s, p).start()
 
+    def begin(g, p):
+        @pl.when(has_up)
+        def _():
+            chain_up(g, r, p).start()
+
+        @pl.when(has_down)
+        def _():
+            chain_down(g, r, p).start()
+
+        for i in ((1, 4), (3, 2))[p]:
+            gather(g, i).start()
+
     current[...] = x_ref[...].astype(f32)
+    rows[0, 0] = x_ref[...]
+    cols[0, r] = x_ref[...]
+    for p in (0, 1):
+        begin(0, p)
+    gather(0, 0).start()
     for g in range(DEGREE):
-        operand = current[...].astype(bf16)
-        rows[g, 0] = operand
-        cols[g, r] = operand
-
-        @pl.when(has_up)
-        def _():
-            for p in (0, 1):
-                chain_up(g, r, p).start()
-
-        @pl.when(has_down)
-        def _():
-            for p in (0, 1):
-                chain_down(g, r, p).start()
-
-        for i in (1, 2, 3, 4, 0):
-            gather(g, i).start()
-        if g == 0:
-            for load in loads:
-                load.wait()
-        mirror_step(g, 0)
-        gather(g, 0).wait_recv()
-        mirror_step(g, 1)
+        if g > 0:
+            gather(g, 0).wait_recv()
+            mirror_step(g, 0, 1)
         for i, onward in ((1, 5), (2, 6)):
             gather(g, i).wait_recv()
             gather(g, onward).start()
         chain_arrive(g, 1, 0)
         if g > 0:
             forward_step(g, r, first=True)
+        else:
+            for load in loads:
+                load.wait()
+            gather(g, 0).wait_recv()
+            mirror_step(g, 0, 1)
         for i, onward in ((3, 7), (4, 8)):
             gather(g, i).wait_recv()
             gather(g, onward).start()
         chain_arrive(g, 1, 1)
-        mirror_step(g, 2)
-        mirror_step(g, 4)
+        mirror_step(g, 2, 4)
         for i, onward in ((5, 9), (6, 10)):
             gather(g, i).wait_recv()
             gather(g, onward).start()
         if n_row > 2:
             chain_arrive(g, 2, 0)
-        for i, j in ((7, 3), (8, 5)):
+        for i in (7, 8):
             gather(g, i).wait_recv()
-            mirror_step(g, j)
+        mirror_step(g, 3, 5)
         mirror_step(g, 6)
         if n_row > 2:
             chain_arrive(g, 2, 1)
@@ -491,36 +496,40 @@
             for p in (0, 1):
                 sum_hop(g, t, p)
         core_copy(g, 1).wait_recv()
-        forward[c] = paired(0)
         for p in (0, 1):
-            forward[c, halves[p]] += mirror_of(r, p)
-        for i in (0, 1):
-            for part in (0, 1):
-                quad_copy(g, i, part).wait_recv()
-        forward[c] += quad_in[g, 0].astype(f32) + quad_in[g, 1].astype(f32)
-
-        @pl.when(has_down)
-        def _():
-            for p in (0, 1):
+            part = halves[p]
+            for i in (0, 1):
+                quad_copy(g, i, p).wait_recv()
+            forward[c, part] += (
+                core_in[g, 0, part].astype(f32) + mirror_of(r, p)
+                + (quad_in[g, 0, part].astype(f32) + quad_in[g, 1, part].astype(f32))
+            )
+
+            @pl.when(has_down)
+            def _():
                 sum_up(g, r, p).wait_recv()
-                forward[c, halves[p]] += up_in[g, r, halves[p]].astype(f32)
-
-        @pl.when(has_up)
-        def _():
-            for p in (0, 1):
+                forward[c, part] += up_in[g, r, part].astype(f32)
+
+            @pl.when(has_up)
+            def _():
                 sum_down(g, r, p).wait_recv()
-                forward[c, halves[p]] += down_in[g, r, halves[p]].astype(f32)
-
-        shifted = forward[c] - center * current[...]
-        if g == 0:
-            following = shifted / half_width
-        else:
-            following = 2.0 * shifted / half_width - previous[...]
-        if g == DEGREE - 1:
-            out_ref[...] = following
-        else:
-            previous[...] = current[...]
-            current[...] = following
+                forward[c, part] += down_in[g, r, part].astype(f32)
+
+            shifted = forward[c, part] - center * current[part]
+            if g == 0:
+                following = shifted / half_width
+            else:
+                following = 2.0 * shifted / half_width - previous[part]
+            if g == DEGREE - 1:
+                out_ref[part] = following
+            else:
+                previous[part] = current[part]
+                current[part] = following
+                rows[g + 1, 0, part] = following.astype(bf16)
+                cols[g + 1, r, part] = following.astype(bf16)
+                begin(g + 1, p)
+        if g < DEGREE - 1:
+            gather(g + 1, 0).start()
 
     for g in range(DEGREE):
         for i in range(len(GATHER)):

time: 97.7 us -> 97.1 us (level)
  no operation moved by 1% of the time
where the time goes in v4:
time: 97.1 us; the launch traced here: 96.8 us
  Pallas kernels  93 us (96%)
  between operations  1.96 us (2%)
  local copies, waits for them, and re-layouts  1.87 us (2%)
    pallas_call x1, Pallas kernels, filter_call(): pl.pallas_call(functools.partial(filter_kernel, n_row, n_col), out_shape=...  86.5 us
    pallas_call x1, Pallas kernels, link_call(): pl.pallas_call(functools.partial(link_kernel, col_blocks), out_shape=(jax...  6.5 us

profile of v4, /device:TPU:0, one launch (start us, length us, event | category | flops | bytes accessed | tf_op | source)
XLA Modules:
  0.0 96.8 jit_solution(8635202554986436645)
XLA Ops:
  1.9 6.5 %link.1 = (s32[512]{0:T(512)}, bf16[128,128,128]{2,1,0:T(8,128)(2,1)}) custom-call(s32[1,1,256]{2,1,0:T(1,128)} %rows_ref.1, s32[1,1,256]{2,1,0:T(1,128)} %cols_ref.1, s32[1,1]{1,0:T(1,128)S(6)} %copy.9.count_ref, bf16[1,1,256,128,128]{4,3,2,1,0:T(8,128)(2,1)} %blocks_hbm.3), custom_call_target="tpu_custom_call" | custom-call | tf_op jit(solution)/shard_map/link/pallas_call | solution.py:162
  8.5 86.5 %filter.1 = f32[512,256]{1,0:T(8,128)} custom-call(bf16[512,256]{1,0:T(8,128)(2,1)} %x_ref.1, f32[1]{0:T(128)S(6)} %copy.10.lower_ref, f32[1]{0:T(128)S(6)} %copy.11.upper_ref, s32[512]{0:T(512)} %get-tuple-element.7.table_ref, bf16[1,1,256,128,128]{4,3,2,1,0:T(8,128)(2,1)} %blocks_hbm.3, bf16[128,128,128]{2,1,0:T(8,128)(2,1)} %get-tuple-element.8.sums_hbm), custom_call_target="tpu_custom_call" | custom-call | tf_op jit(solution)/shard_map/filter/pallas_call | solution.py:591
  94.9 1.9 %copy.12 = f32[512,256]{1,0:T(8,128)} copy(f32[512,256]{1,0:T(8,128)} %filter.1) | data formatting | bytes 1048576

commit v5 on v4

--- a/solution.py
+++ b/solution.py
@@ -295,7 +295,7 @@
                 ] = pool[table_ref[first + k]]
             return carry
 
-        lax.fori_loop(0, per_seg * n_row, one, 0)
+        lax.fori_loop(0, per_seg * n_row, one, 0, unroll=4)
 
     def mirror_step(g, *slots_here):
         segments = [peer(j) for j in slots_here]
@@ -314,7 +314,7 @@
                 mirror_t[s] += product
             return carry
 
-        lax.fori_loop(0, n_row, one, 0)
+        lax.fori_loop(0, n_row, one, 0, unroll=n_row)
 
     def forward_step(g, q, first=False):
         def one(a, carry):
@@ -325,7 +325,7 @@
                 forward[a] += product
             return carry
 
-        lax.fori_loop(0, n_col, one, 0)
+        lax.fori_loop(0, n_col, one, 0, unroll=4)
 
     q_last = jnp.where(2 * r < n_row, n_row - 1, 0)
 

time: 97.1 us -> 88.2 us (0.908)
  Pallas kernels: 93 us -> 83.9 us
    pallas_call x1, Pallas kernels: 86.5 us -> 77.8 us  [filter_call(): pl.pallas_call(functools.partial(filter_kernel, n_row, n_col), out_shape=...]
where the time goes in v5:
time: 88.2 us; the launch traced here: 87.7 us
  Pallas kernels  83.9 us (95%)
  between operations  1.96 us (2%)
  local copies, waits for them, and re-layouts  1.87 us (2%)
    pallas_call x1, Pallas kernels, filter_call(): pl.pallas_call(functools.partial(filter_kernel, n_row, n_col), out_shape=...  77.8 us
    pallas_call x1, Pallas kernels, link_call(): pl.pallas_call(functools.partial(link_kernel, col_blocks), out_shape=(jax...  6.11 us
    unnamed x1, local copies, waits for them, and re-layouts  1.87 us

profile of v5, /device:TPU:0, one launch (start us, length us, event | category | flops | bytes accessed | tf_op | source)
XLA Modules:
  0.0 87.7 jit_solution(12642875348688506637)
XLA Ops:
  1.9 6.1 %link.1 = (s32[512]{0:T(512)}, bf16[128,128,128]{2,1,0:T(8,128)(2,1)}) custom-call(s32[1,1,256]{2,1,0:T(1,128)} %rows_ref.1, s32[1,1,256]{2,1,0:T(1,128)} %cols_ref.1, s32[1,1]{1,0:T(1,128)S(6)} %copy.9.count_ref, bf16[1,1,256,128,128]{4,3,2,1,0:T(8,128)(2,1)} %blocks_hbm.3), custom_call_target="tpu_custom_call" | custom-call | tf_op jit(solution)/shard_map/link/pallas_call | solution.py:162
  8.1 77.8 %filter.1 = f32[512,256]{1,0:T(8,128)} custom-call(bf16[512,256]{1,0:T(8,128)(2,1)} %x_ref.1, f32[1]{0:T(128)S(6)} %copy.10.lower_ref, f32[1]{0:T(128)S(6)} %copy.11.upper_ref, s32[512]{0:T(512)} %get-tuple-element.7.table_ref, bf16[1,1,256,128,128]{4,3,2,1,0:T(8,128)(2,1)} %blocks_hbm.3, bf16[128,128,128]{2,1,0:T(8,128)(2,1)} %get-tuple-element.8.sums_hbm), custom_call_target="tpu_custom_call" | custom-call | tf_op jit(solution)/shard_map/filter/pallas_call | solution.py:591
  85.8 1.9 %copy.12 = f32[512,256]{1,0:T(8,128)} copy(f32[512,256]{1,0:T(8,128)} %filter.1) | data formatting | bytes 1048576
